TPU v7x, 32 devices: a whole 2x2x4 slice. The times are simulated.
32 devices in a mesh: req: 2 (over x), ctx: 16 (over z, y, core).
Axes of the slice: x: 2, y: 2, z: 4, core: 2. Of those that a mesh axis runs over, the one named last changes fastest.
Arguments:
- hidden: bfloat16 [512, 8192], P(('req', 'ctx')), parts along dimension 0, may hold values from -6 to 6
- keep_order: int32 [32, 16], P('req'), parts along dimension 0, may hold values from 0 to 15, each once within a row
- keep_count: int32 [32], P('req'), parts along dimension 0, may hold values from 1 to 4, 32 in all
- positions: int32 [512], P('req'), parts along dimension 0, may hold values from 130561 to 131071, as said below
- w_query: bfloat16 [8192, 8192], P(None, 'ctx'), may hold values from -0.0625 to 0.0625
- w_keyval: bfloat16 [8192, 2048], P(None, 'ctx'), may hold values from -0.25 to 0.25
- cache: bfloat16 [32768, 2048], P(('req', 'ctx')), parts along dimension 0, may hold values from -520 to 520, as said below
Outputs:
- attended: bfloat16 [64, 8192], P('req', 'ctx'), parts along dimension 0
There are 2 independent parts, one for each index of `req`. A program takes and returns all parts, laid end to end along the dimension named above; an argument that names none is the same for every part. Nothing has to cross between parts.
Inputs may be any that keep to these rules, and one draw needn't show every extreme that they name: `keep_order`: each row lists every local index once; a shard's first keep_count entries are its kept tokens. `keep_count`: the counts sum to 32. `positions`: rising by 1 or 2 from token to token; the last token has position 131071. `cache`: keys are already rotated.
All inputs are finite; a program needn't handle non-finite values.
Results may differ from a plain program's by a relative error of at most 0.018.
The roundings to bfloat16 on the way count: a program that leaves them out, or rounds other values in their place, can miss the bound.
Values may be sent and summed in bfloat16 or wider, within the bound.
A program may use at most 64 MiB of HBM per device.

v0:
```python
import math

import jax
import jax.numpy as jnp
from jax import lax
from jax.sharding import PartitionSpec as P

H = 64
KVH = 8
HD = 128
KEEP_DEV = 2
KMAX = 4


def rope_table(head_size):
    half = head_size // 2
    period = 2.0 * math.pi
    scaled_list = []
    wrapped_list = []
    for column in range(half):
        inverse = 500000.0 ** (-2.0 * column / head_size)
        wavelen = 2.0 * math.pi / inverse
        if wavelen > 8192.0:
            scaled_rate = inverse / 8.0
        elif wavelen < 2048.0:
            scaled_rate = inverse
        else:
            smooth = (8192.0 / wavelen - 1.0) / 3.0
            scaled_rate = (1.0 - smooth) * inverse / 8.0 + smooth * inverse
        scaled_list.append(scaled_rate)
        step_angle = 1024.0 * scaled_rate
        wrapped_list.append(step_angle - period * (step_angle // period))
    return (jnp.asarray(scaled_list, jnp.float32), jnp.asarray(wrapped_list, jnp.float32))


def rotate(values, places):
    scaled, wrapped = rope_table(values.shape[-1])
    upper = (places // 1024).astype(jnp.float32)
    lower = (places % 1024).astype(jnp.float32)
    angle = lower[:, None] * scaled[None, :] + upper[:, None] * wrapped[None, :]
    cosine = jnp.cos(angle)[:, None, :]
    sine = jnp.sin(angle)[:, None, :]
    half = values.shape[-1] // 2
    first = values[..., :half]
    second = values[..., half:]
    return jnp.concatenate(
        [first * cosine - second * sine, second * cosine + first * sine], axis=-1
    )


def kept_sources(keep_count, kept_total, shards):
    ends = jnp.cumsum(keep_count)
    starts = ends - keep_count
    slots = jnp.arange(kept_total, dtype=jnp.int32)
    owner = jnp.sum((ends[None, :] <= slots[:, None]).astype(jnp.int32), axis=1)
    ids = jnp.arange(shards, dtype=jnp.int32)
    first = jnp.sum(jnp.where(ids[None, :] == owner[:, None], starts[None, :], 0), axis=1)
    return (owner, slots - first)


def body(hidden, keep_order, keep_count, positions, w_query, w_keyval, cache):
    shards = lax.axis_size("ctx")
    me = lax.axis_index("ctx")
    span_rows = hidden.shape[0]
    kept_total = KEEP_DEV * shards
    block = KEEP_DEV
    cache_rows = cache.shape[0]
    heads_here = H // shards
    order_here = lax.dynamic_slice_in_dim(keep_order, me, 1, 0)[0, :KMAX]
    slot_rows = hidden[order_here]
    rows_all = lax.all_gather(slot_rows, "ctx", axis=0, tiled=True)
    owner, local = kept_sources(keep_count, kept_total, shards)
    rows = rows_all[owner * KMAX + local]
    places = positions[owner * span_rows + keep_order[owner, local]]
    query = jnp.dot(rows, w_query, preferred_element_type=jnp.float32).reshape(
        kept_total, heads_here, HD
    )
    query = rotate(query, places).astype(jnp.bfloat16).reshape(kept_total, heads_here * HD)
    key_part = jnp.dot(rows, w_keyval, preferred_element_type=jnp.float32).astype(jnp.bfloat16)
    own_keyval = lax.all_to_all(key_part, "ctx", split_axis=0, concat_axis=1, tiled=True)
    own_places = lax.dynamic_slice_in_dim(places, me * block, block, 0)
    new_keys = rotate(
        own_keyval[:, : KVH * HD].astype(jnp.float32).reshape(block, KVH, HD), own_places
    )
    new_keys = new_keys.astype(jnp.bfloat16).reshape(block, KVH * HD)
    keys = jnp.concatenate([cache[:, : KVH * HD], new_keys], axis=0)
    values = jnp.concatenate([cache[:, KVH * HD :], own_keyval[:, KVH * HD :]], axis=0)
    queries = lax.all_gather(query, "ctx", axis=1, tiled=True)
    visible = jnp.concatenate(
        [jnp.ones((kept_total, cache_rows), bool), own_places[None, :] <= places[:, None]], axis=1
    )
    group = H // KVH
    scale = 1.0 / math.sqrt(HD)
    numer_list = []
    top_list = []
    total_list = []
    for index in range(KVH):
        q_group = queries[:, index * group * HD : (index + 1) * group * HD].reshape(
            kept_total, group, HD
        )
        k_group = keys[:, index * HD : (index + 1) * HD]
        v_group = values[:, index * HD : (index + 1) * HD]
        scores = (
            jnp.einsum("qhd,kd->qhk", q_group, k_group, preferred_element_type=jnp.float32) * scale
        )
        scores = jnp.where(visible[:, None, :], scores, -1e30)
        top = jnp.max(scores, axis=2)
        weights = jnp.exp(scores - top[..., None])
        total_list.append(jnp.sum(weights, axis=2))
        top_list.append(top)
        numer = jnp.einsum(
            "qhk,kd->qhd", weights.astype(jnp.bfloat16), v_group, preferred_element_type=jnp.float32
        )
        numer_list.append(numer.reshape(kept_total, group * HD))
    numer = jnp.concatenate(numer_list, axis=1)
    top = jnp.concatenate(top_list, axis=1)
    total = jnp.concatenate(total_list, axis=1)
    best = lax.pmax(top.astype(jnp.bfloat16), "ctx").astype(top.dtype)
    factor = jnp.exp(top - best)
    scaled_numer = (numer.reshape(kept_total, H, HD) * factor[..., None]).reshape(
        kept_total, H * HD
    )
    result, denom = (
        lax.psum_scatter(scaled_numer, "ctx", scatter_dimension=1, tiled=True),
        lax.psum_scatter(total * factor, "ctx", scatter_dimension=1, tiled=True),
    )
    result = result.reshape(kept_total, heads_here, HD)
    return (result / denom[..., None]).reshape(kept_total, heads_here * HD).astype(jnp.bfloat16)


def solution(mesh):
    return jax.shard_map(
        body,
        mesh=mesh,
        in_specs=(
            P(("req", "ctx"), None),
            P("req", None),
            P("req"),
            P("req"),
            P(None, "ctx"),
            P(None, "ctx"),
            P(("req", "ctx"), None),
        ),
        out_specs=P("req", "ctx"),
        check_vma=False,
    )
```

profile of v0, /device:TPU:0, one launch (start us, length us, event | category | flops | bytes accessed | tf_op | source)
XLA Modules:
  0.0 212.9 jit_solution(12634720295644664534)
XLA Ops:
  9.2 1.4 gather_fusion
  10.6 2.3 %gather_fusion.2 = bf16[4,8192]{1,0:T(4,128)(2,1)} fusion(bf16[16,8192]{1,0:T(8,128)(2,1)} %param.11, s32[1024]{0:T(1024)S(1)} %get-tuple-element.49), kind=kCustom, calls=%fused_computation.2 | custom fusion | bytes 131088 | tf_op jit(solution)/shard_map/gather | solution.py:70
  14.2 4.6 %fusion.124 = (bf16[1024,1024]{1,0:T(8,128)(2,1)}, bf16[1024,1024]{1,0:T(8,128)(2,1)}) fusion(bf16[1024,2048]{1,0:T(8,128)(2,1)} %param.17), kind=kLoop, calls=%fused_computation.212 | loop fusion | bytes 8388608 | tf_op jit(solution)/shard_map/slice | solution.py:87
  18.7 35.0 %all-gather.4.cloned.1.call-done = bf16[16,4,8192]{2,1,0:T(4,128)(2,1)} async-done(((bf16[1,4,8192]{2,1,0:T(4,128)(2,1)}), bf16[16,4,8192]{2,1,0:T(4,128)(2,1)}) %all-gather.4.cloned.1.call-update) | async-done | bytes 1048592 | tf_op jit(solution)/shard_map/all_gather | solution.py:71
  53.7 1.3 reshape.473
  55.0 1.7 gather_fusion.3
  56.7 2.2 %convolution_convert_fusion = bf16[32,128]{1,0:T(8,128)(2,1)} fusion(bf16[32,8192]{1,0:T(8,128)(2,1)} %gather_fusion.3, bf16[8192,128]{1,0:T(8,128)(2,1)S(1)} %copy-done), kind=kOutput, calls=%fused_computation.50 | convolution fusion | flops 67112960 | bytes 2629632 | tf_op jit(solution)/shard_map/dot_general | solution.py:79
  58.9 4.9 %fusion.134 = f32[32,512]{1,0:T(8,128)S(1)} fusion(bf16[32,8192]{1,0:T(8,128)(2,1)S(1)} %copy-done.6, bf16[8192,512]{1,0:T(8,128)(2,1)} %param.15), kind=kOutput, calls=%fused_computation.222 | convolution fusion | flops 268435456 | bytes 8978432 | tf_op jit(solution)/shard_map/dot_general | solution.py:75
  64.1 3.6 %all-to-all-start = ((bf16[16,2,128]{2,1,0:T(2,128)(2,1)}), bf16[16,2,128]{2,1,0:T(2,128)(2,1)S(1)}, u32[]{:S(2)}, u32[]{:S(2)}) async-start(bf16[16,2,128]{2,1,0:T(2,128)(2,1)} %bitcast.10), calls=%async_computation | async-start | bytes 16384 | tf_op jit(solution)/shard_map/all_to_all | solution.py:80
  67.8 23.4 %all_gather.7 = bf16[32,8192]{1,0:T(8,128)(2,1)S(1)} all-gather(bf16[32,512]{1,0:T(8,128)(2,1)S(1)} %bitcast.184), channel_id=1, replica_groups=mesh['req'=2,'ctx'=16] {'ctx'}, dimensions={1}, use_global_device_ids=true | all-gather | bytes 557056 | tf_op jit(solution)/shard_map/all_gather | solution.py:88
  92.2 1.6 fusion.126
  97.1 0.9 fusion.12
  98.9 0.9 fusion.14
  100.7 0.9 fusion.16
  102.5 0.9 fusion.18
  104.8 1.4 fusion.132
  106.3 1.7 fusion.20
  108.0 2.2 %convolution_dynamic-update-slice_fusion.1 = f32[32,64,128]{2,1,0:T(8,128)} fusion(f32[32,64,128]{2,1,0:T(8,128)} %copy-done.7, f32[32,8,1026]{2,1,0:T(8,128)S(1)} %copy-done.5, f32[32,8]{1,0:T(8,128)S(1)} %get-tuple-element.45, bf16[1024,1024]{1,0:T(8,128)(2,1)} %get-tuple-element.9, bf16[2,1024]{1,0:T(2,128)(2,1)S(1)} %get-tuple-element.23), kind=kOutput, calls=%fused_computation.43 | convolution fusion | flops 68290560 | bytes 3283968 | tf_op jit(solution)/shard_map/qhk,kd->qhd/dot_general | solution.py:111
  110.5 1.0 convolution_dynamic-update-slice_fusion
  111.6 30.4 %pmax.7 = bf16[32,64]{1,0:T(8,128)(2,1)S(1)} all-reduce(bf16[32,64]{1,0:T(8,128)(2,1)S(1)} %convert_element_type.86), channel_id=1, replica_groups=mesh['req'=2,'ctx'=16] {'ctx'}, use_global_device_ids=true, to_apply=%region_11.12 | all-reduce | flops 2048 | bytes 8192 | tf_op jit(solution)/shard_map/pmax | solution.py:118
  142.1 1.6 broadcast_multiply_fusion
  143.7 1.6 copy.35
  146.6 57.9 %all-reduce.1 = f32[32,64]{1,0:T(8,128)S(1)} all-reduce(f32[32,64]{1,0:T(8,128)S(1)} %get-tuple-element.5), channel_id=4, replica_groups=mesh['req'=2,'ctx'=16] {'ctx'}, use_global_device_ids=true, to_apply=%region_21.22.clone | all-reduce | flops 2048 | bytes 16384
  204.6 1.5 fusion.88
  (98 shorter events, 13.6 us)
Async XLA Ops:
  6.5 50.2 %copy-start = (bf16[8192,128]{1,0:T(8,128)(2,1)S(1)}, bf16[8192,128]{1,0:T(8,128)(2,1)}, u32[]{:S(2)}) copy-start(bf16[8192,128]{1,0:T(8,128)(2,1)} %param.16) | copy-start | bytes 6291460
  6.5 7.3 %copy-start.13 = (f32[64]{0:T(128)S(1)}, f32[64]{0:T(128)}, u32[]{:S(2)}) copy-start(f32[64]{0:T(128)} %constant.84.clone) | copy-start | bytes 772
  6.5 7.3 %copy-start.14 = (f32[64]{0:T(128)S(1)}, f32[64]{0:T(128)}, u32[]{:S(2)}) copy-start(f32[64]{0:T(128)} %constant.83.clone) | copy-start | bytes 772
  6.5 6.4 %copy-start.1 = (s32[256]{0:T(256)S(1)}, s32[256]{0:T(256)}, u32[]{:S(2)}) copy-start(s32[256]{0:T(256)} %param.14) | copy-start | bytes 3076
  6.5 47.2 %all-gather.4.cloned.1.call-start = ((), (), s32[]{:S(2)}) async-start(), calls=%async_computation.3 | async-start | bytes 1114112 | tf_op jit(solution)/shard_map/all_gather | solution.py:71
  56.7 2.2 %copy-start.6 = (bf16[32,8192]{1,0:T(8,128)(2,1)S(1)}, bf16[32,8192]{1,0:T(8,128)(2,1)}, u32[]{:S(2)}) copy-start(bf16[32,8192]{1,0:T(8,128)(2,1)} %gather_fusion.3) | copy-start | bytes 1572868
  64.1 27.9 %all-to-all-start = ((bf16[16,2,128]{2,1,0:T(2,128)(2,1)}), bf16[16,2,128]{2,1,0:T(2,128)(2,1)S(1)}, u32[]{:S(2)}, u32[]{:S(2)}) async-start(bf16[16,2,128]{2,1,0:T(2,128)(2,1)} %bitcast.10), calls=%async_computation | async-start | bytes 16384 | tf_op jit(solution)/shard_map/all_to_all | solution.py:80
  67.7 136.8 %reduce-scatter.3.cloned.1.call-start = ((), (), s32[]{:S(2)}) async-start(), calls=%async_computation.2 | async-start | bytes 1114112 | tf_op jit(solution)/shard_map/reduce_scatter | solution.py:124
  92.2 1.7 copy-start.4
  93.9 1.6 copy-start.2
  103.4 0.8 copy-start.8
  103.8 2.4 %copy-start.7 = (f32[32,64,128]{2,1,0:T(8,128)}, f32[32,64,128]{2,1,0:T(8,128)S(1)}, u32[]{:S(2)}) copy-start(f32[32,64,128]{2,1,0:T(8,128)S(1)} %convolution_dynamic-update-slice_fusion.2) | copy-start | bytes 3145732
  106.3 1.7 copy-start.5
  108.0 2.5 %copy-start.3 = (bf16[1024,1024]{1,0:T(8,128)(2,1)S(1)}, bf16[1024,1024]{1,0:T(8,128)(2,1)}, u32[]{:S(2)}) copy-start(bf16[1024,1024]{1,0:T(8,128)(2,1)} %get-tuple-element.9) | copy-start | bytes 6291460
  110.5 31.5 %copy-start.9 = (f32[32,8]{1,0:T(8,128)S(1)}, f32[32,8]{1,0:T(8,128)}, u32[]{:S(2)}) copy-start(f32[32,8]{1,0:T(8,128)} %fusion.12) | copy-start | bytes 3076
  110.5 31.5 %copy-start.10 = (f32[32,8]{1,0:T(8,128)S(1)}, f32[32,8]{1,0:T(8,128)}, u32[]{:S(2)}) copy-start(f32[32,8]{1,0:T(8,128)} %fusion.14) | copy-start | bytes 3076
  110.5 31.5 %copy-start.11 = (f32[32,8]{1,0:T(8,128)S(1)}, f32[32,8]{1,0:T(8,128)}, u32[]{:S(2)}) copy-start(f32[32,8]{1,0:T(8,128)} %fusion.16) | copy-start | bytes 3076
  110.5 31.5 %copy-start.12 = (f32[32,8]{1,0:T(8,128)S(1)}, f32[32,8]{1,0:T(8,128)}, u32[]{:S(2)}) copy-start(f32[32,8]{1,0:T(8,128)} %fusion.18) | copy-start | bytes 3076
  143.7 1.6 copy-start.15
Sparse Core Ops, SparseCore 0:
  13.0 40.6 all-gather.3
  145.4 54.6 reduce-scatter.2
where the time goes:
time: 214 us; the launch traced here: 213 us
  blocking collectives  112 us (52%)
  waiting for transfers between devices  35 us (16%)
  matrix products  18.6 us (9%)
  local copies, waits for them, and re-layouts  18.3 us (9%)
  between operations  14.5 us (7%)
  other arithmetic  11.1 us (5%)
  starting transfers between devices  3.71 us (2%)
    unnamed x1, blocking collectives  57.9 us
    all_gather x1, waiting for transfers between devices, body(): rows_all = lax.all_gather(slot_rows, 'ctx', axis=0, tiled=True)  35 us
    pmax x1, blocking collectives, body(): best = lax.pmax(top.astype(jnp.bfloat16), 'ctx').astype(top.dtype)  30.4 us
    all_gather x1, blocking collectives, body(): queries = lax.all_gather(query, 'ctx', axis=1, tiled=True)  23.4 us
    reduce_sum x8, other arithmetic, body(): total_list.append(jnp.sum(weights, axis=2))  6.26 us
    dot_general x8, matrix products, body(): jnp.einsum('qhd,kd->qhk', q_group, k_group, preferred_element_type=jnp.fl...  6.03 us
    unnamed x48, local copies, waits for them, and re-layouts  5.71 us
    dot_general x8, matrix products, body(): jnp.einsum('qhk,kd->qhd', weights.astype(jnp.bfloat16), v_group, preferre...  5.5 us
  transfers between devices with their start and end apart: 3, of which 1 were waited for; matrix products, arithmetic and copies ran while one was open for 3% of the time, Pallas kernels for 0%

commit v1 on v0

--- a/solution.py
+++ b/solution.py
@@ -1,8 +1,11 @@
+import functools
 import math
 
 import jax
 import jax.numpy as jnp
 from jax import lax
+from jax.experimental import pallas as pl
+from jax.experimental.pallas import tpu as pltpu
 from jax.sharding import PartitionSpec as P
 
 H = 64
@@ -128,9 +131,366 @@
     return (result / denom[..., None]).reshape(kept_total, heads_here * HD).astype(jnp.bfloat16)
 
 
+MESH = pl.DeviceIdType.MESH
+ZS = 4
+SHARDS = 16
+KEEP = 32
+GROUPS = 4
+WIDE = 2048
+QROWS = 128
+EXP2_SCALE = math.log2(math.e) / math.sqrt(HD)
+MSG = QROWS + 16
+
+
+def pack(ref, index, partial, lse):
+    ref[index, :QROWS, :] = partial.astype(jnp.bfloat16)
+    high = lse.astype(jnp.bfloat16).astype(jnp.float32)
+    middle = (lse - high).astype(jnp.bfloat16).astype(jnp.float32)
+    low = lse - high - middle
+    row = lax.broadcasted_iota(jnp.int32, (16, QROWS), 0)
+    stats = jnp.where(row == 0, high, jnp.where(row == 1, middle, jnp.where(row == 2, low, 0.0)))
+    ref[index, QROWS:, :] = stats.astype(jnp.bfloat16)
+
+
+def unpack(ref, index):
+    stats = ref[index, QROWS:, :].astype(jnp.float32)
+    return ref[index, :QROWS, :].astype(jnp.float32), jnp.sum(stats, axis=0, keepdims=True)
+
+
+def merge(pieces):
+    best = functools.reduce(jnp.maximum, [lse for _, lse in pieces])
+    factors = [jnp.exp2(lse - best) for _, lse in pieces]
+    total = sum(factors)
+    inverse = 1.0 / total
+    mixed = sum(partial * (factor * inverse) for (partial, _), factor in zip(pieces, factors))
+    return mixed, best + jnp.log2(total)
+
+
+def contract(a, b, dims):
+    return lax.dot_general(a, b, ((dims[:1], dims[1:]), ((), ())), preferred_element_type=jnp.float32)
+
+
+def kernel(
+    order, count, pos, table, hidden, w_query, w_keyval, cache, out,
+    hidden_v, query_v, keyval_v, cache_v, slots, qbuf, values_t,
+    own, own_lse, send_s, recv_s, send_y, recv_y, send_z, recv_z,
+    load_sem, row_send, row_recv, q_send, q_recv,
+    s_send, s_recv, y_send, y_recv, z_send, z_recv,
+):
+    me = lax.axis_index("ctx")
+    z = me // 4
+    y = (me // 2) % 2
+    c = me % 2
+    sibling = me + 1 - 2 * c
+    y_peer = me + 2 - 4 * y
+
+    def z_at(dz):
+        return (z + dz) % ZS
+
+    def z_peer(dz):
+        return z_at(dz) * 4 + me % 4
+
+    def block_at(dz, dy, dc):
+        yy = y if dy == 0 else 1 - y
+        cc = c if dc == 0 else 1 - c
+        return z_at(dz) * 4 + yy * 2 + cc
+
+    loads = [
+        pltpu.make_async_copy(hidden, hidden_v, load_sem.at[0]),
+        pltpu.make_async_copy(w_query, query_v, load_sem.at[1]),
+        pltpu.make_async_copy(w_keyval, keyval_v, load_sem.at[2]),
+        pltpu.make_async_copy(cache, cache_v, load_sem.at[3]),
+    ]
+    for load in loads:
+        load.start()
+
+    barrier = pltpu.get_barrier_semaphore()
+    peers = [sibling, y_peer] + [z_peer(dz) for dz in (1, 2, 3)]
+    for peer in peers:
+        pl.semaphore_signal(barrier, inc=1, device_id={"ctx": peer}, device_id_type=MESH)
+
+    row = lax.broadcasted_iota(jnp.int32, (16, 16), 0)
+    column = lax.broadcasted_iota(jnp.int32, (16, 16), 1)
+    chosen = jnp.zeros((16, 16), jnp.int32)
+    for slot in range(KMAX):
+        chosen = jnp.where(row % 4 == slot, order[me, slot], chosen)
+    loads[0].wait()
+    picked = jnp.zeros((16, WIDE), jnp.float32)
+    for g in range(GROUPS):
+        onehot = jnp.where((chosen == column) & (row // 4 == g), 1.0, 0.0).astype(jnp.bfloat16)
+        picked += contract(onehot, hidden_v[:, g * WIDE : (g + 1) * WIDE], (1, 0))
+    slots[me] = picked.astype(jnp.bfloat16)
+    pl.semaphore_wait(barrier, len(peers))
+
+    def relay(buf, send_sem, recv_sem, between):
+        sent = []
+
+        def send(at, receiver_at, peer):
+            copy = pltpu.make_async_remote_copy(
+                src_ref=buf.at[block_at(*at)],
+                dst_ref=buf.at[block_at(*at)],
+                send_sem=send_sem.at[len(sent)],
+                recv_sem=recv_sem.at[receiver_at],
+                device_id={"ctx": peer},
+                device_id_type=MESH,
+            )
+            copy.start()
+            sent.append(copy)
+
+        def arrived(dz, dy, dc):
+            pltpu.make_async_remote_copy(
+                src_ref=buf.at[block_at(dz, dy, dc)],
+                dst_ref=buf.at[block_at(dz, dy, dc)],
+                send_sem=send_sem.at[0],
+                recv_sem=recv_sem.at[dz * 4 + dy * 2 + dc],
+                device_id={"ctx": sibling},
+                device_id_type=MESH,
+            ).wait_recv()
+
+        for dz in (2, 1, 3):
+            send((0, 0, 0), (ZS - dz) * 4, z_peer(dz))
+        send((0, 0, 0), 2, y_peer)
+        send((0, 0, 0), 1, sibling)
+        result = between()
+        for dz in (1, 3, 2):
+            arrived(dz, 0, 0)
+            send((dz, 0, 0), dz * 4 + 2, y_peer)
+            send((dz, 0, 0), dz * 4 + 1, sibling)
+        for dz in (0, 1, 3, 2):
+            arrived(dz, 1, 0)
+            send((dz, 1, 0), dz * 4 + 3, sibling)
+        for dy in (0, 1):
+            for dz in (0, 1, 3, 2):
+                arrived(dz, dy, 1)
+        return sent, result
+
+    def tables():
+        lane = lax.broadcasted_iota(jnp.int32, (1, 256), 1)
+        source = lane // 16
+        local = lane % 4
+        first = jnp.zeros((1, 256), jnp.int32)
+        kept = jnp.zeros((1, 256), jnp.int32)
+        place = jnp.zeros((1, 256), jnp.int32)
+        begin = jnp.int32(0)
+        for s in range(SHARDS):
+            first = jnp.where(source == s, begin, first)
+            kept = jnp.where(source == s, count[s], kept)
+            begin = begin + count[s]
+            for slot in range(KMAX):
+                place = jnp.where(
+                    (source == s) & (local == slot), pos[s * 16 + order[s, slot]], place
+                )
+        target = jnp.where(local < kept, first + local, -1)
+        listed = lax.broadcasted_iota(jnp.int32, (KEEP, 256), 0) == target
+        group = (lane // 4) % 4
+        picks = [
+            jnp.where(listed & (group == g), 1.0, 0.0).astype(jnp.bfloat16) for g in range(GROUPS)
+        ]
+        mine = jnp.where(listed & (group == 0), 1.0, 0.0)
+        upper = jnp.sum(mine * (place >> 10).astype(jnp.float32), axis=1, keepdims=True)
+        lower = jnp.sum(mine * (place & 1023).astype(jnp.float32), axis=1, keepdims=True)
+        angle = lower * table[0:1, :] + upper * table[1:2, :]
+        return picks, upper * 1024.0 + lower, jnp.cos(angle), jnp.sin(angle) * table[2:3, :]
+
+    def before_rows():
+        result = tables()
+        loads[3].wait()
+        return result
+
+    row_sent, (picks, places, cosine, sine) = relay(slots, row_send, row_recv, before_rows)
+    loads[1].wait()
+    loads[2].wait()
+    query = jnp.zeros((KEEP, 4 * HD), jnp.float32)
+    keyval = jnp.zeros((KEEP, HD), jnp.float32)
+    for g in range(GROUPS):
+        rows = contract(picks[g], slots[...].reshape(256, WIDE), (1, 0)).astype(jnp.bfloat16)
+        query += contract(rows, query_v[g * WIDE : (g + 1) * WIDE, :], (1, 0))
+        keyval += contract(rows, keyval_v[g * WIDE : (g + 1) * WIDE, :], (1, 0))
+
+    def turn(part):
+        return part * cosine + pltpu.roll(part, HD // 2, 1) * sine
+
+    for h in range(4):
+        qbuf[me, h * KEEP : (h + 1) * KEEP, :] = turn(query[:, h * HD : (h + 1) * HD]).astype(
+            jnp.bfloat16
+        )
+    plain = keyval.astype(jnp.bfloat16).astype(jnp.float32)
+    qbuf[me, QROWS:, :] = jnp.where(me < KVH, turn(plain), plain).astype(jnp.bfloat16)
+
+    def before_queries():
+        for g in range(KVH):
+            at = (KVH + g) * HD
+            values_t[g] = cache_v[:, at : at + HD].T
+
+    q_sent, _ = relay(qbuf, q_send, q_recv, before_queries)
+
+    def attend(g):
+        keys = cache_v[:, pl.ds(pl.multiple_of(g * HD, HD), HD)]
+        both = jnp.concatenate(
+            [qbuf[2 * g + 1 - c, :QROWS, :], qbuf[2 * g + c, :QROWS, :]], axis=0
+        )
+        scores = contract(keys, both, (1, 1))
+        top = jnp.max(scores, axis=0, keepdims=True)
+        weights = jnp.exp2((scores - top) * EXP2_SCALE)
+        total = jnp.sum(weights, axis=0, keepdims=True)
+        numer = contract(values_t[g], weights.astype(jnp.bfloat16), (1, 0))
+        partial = numer * (1.0 / total)
+        lse = top * EXP2_SCALE + jnp.log2(total)
+        pack(send_s, g, partial[:, :QROWS], lse[:, :QROWS])
+        own[g] = partial[:, QROWS:]
+        own_lse[g] = jnp.broadcast_to(lse[:, QROWS:], (8, QROWS))
+
+    def move(src, dst, index_from, index_to, ssem, rsem, peer):
+        return pltpu.make_async_remote_copy(
+            src_ref=src.at[index_from],
+            dst_ref=dst.at[index_to],
+            send_sem=ssem,
+            recv_sem=rsem,
+            device_id={"ctx": peer},
+            device_id_type=MESH,
+        )
+
+    def to_sibling(dz, dy):
+        g = z_at(dz) * 2 + (y if dy == 0 else 1 - y)
+        at = dz * 2 + dy
+        return move(send_s, recv_s, g, g, s_send.at[at], s_recv.at[at], sibling)
+
+    def to_y(dz):
+        return move(send_y, recv_y, dz, dz, y_send.at[dz], y_recv.at[dz], y_peer)
+
+    def to_z(dz):
+        return move(send_z, recv_z, dz, ZS - dz, z_send.at[dz], z_recv.at[ZS - dz], z_peer(dz))
+
+    def mine_and_sibling(dz, dy):
+        g = z_at(dz) * 2 + (y if dy == 0 else 1 - y)
+        to_sibling(dz, dy).wait_recv()
+        return [(own[g], own_lse[g, 0:1, :]), unpack(recv_s, g)]
+
+    turns = [(dz, dy) for dz in (2, 1, 3, 0) for dy in (1, 0)]
+
+    def follow(dz, dy):
+        if dy == 1:
+            pack(send_y, dz, *merge(mine_and_sibling(dz, 1)))
+            to_y(dz).start()
+            return None
+        pieces = mine_and_sibling(dz, 0)
+        to_y(dz).wait_recv()
+        pieces.append(unpack(recv_y, dz))
+        if dz == 0:
+            return merge(pieces)
+        pack(send_z, dz, *merge(pieces))
+        to_z(dz).start()
+        return None
+
+    lag = 1
+    local = None
+    for step in range(len(turns) + lag):
+        if step < len(turns):
+            dz, dy = turns[step]
+            attend(z_at(dz) * 2 + (y if dy == 0 else 1 - y))
+            to_sibling(dz, dy).start()
+        if step == len(turns) - 1:
+            new_keys = qbuf[me // 2, QROWS:, :]
+            new_values = qbuf[KVH + me // 2, QROWS:, :]
+            spot = lax.broadcasted_iota(jnp.int32, (KEEP, QROWS), 0)
+            lane = lax.broadcasted_iota(jnp.int32, (KEEP, QROWS), 1)
+            asker = jnp.sum(jnp.where(lane % KEEP == spot, places, 0.0), axis=0, keepdims=True)
+            scores = contract(new_keys, qbuf[me, :QROWS, :], (1, 1))
+            seen = places <= asker
+            scores = jnp.where(seen, scores, -1e30)
+            top = jnp.max(scores, axis=0, keepdims=True)
+            weights = jnp.where(seen, jnp.exp2((scores - top) * EXP2_SCALE), 0.0)
+            total = jnp.sum(weights, axis=0, keepdims=True)
+            numer = contract(new_values, weights.astype(jnp.bfloat16), (0, 0))
+            fresh = (numer * (1.0 / total), top * EXP2_SCALE + jnp.log2(total))
+        if step >= lag:
+            local = follow(*turns[step - lag])
+
+    pieces = [local, fresh]
+    for dz in (1, 3, 2):
+        pltpu.make_async_remote_copy(
+            src_ref=send_z.at[dz],
+            dst_ref=recv_z.at[dz],
+            send_sem=z_send.at[dz],
+            recv_sem=z_recv.at[dz],
+            device_id={"ctx": z_peer(dz)},
+            device_id_type=MESH,
+        ).wait_recv()
+        pieces.append(unpack(recv_z, dz))
+    mixed, _ = merge(pieces)
+    final = mixed.T
+    for h in range(4):
+        out[:, h * HD : (h + 1) * HD] = final[h * KEEP : (h + 1) * KEEP, :].astype(jnp.bfloat16)
+
+    for copy in row_sent + q_sent:
+        copy.wait_send()
+    for dz, dy in turns:
+        to_sibling(dz, dy).wait_send()
+    for dz in range(ZS):
+        to_y(dz).wait_send()
+    for dz in (1, 2, 3):
+        to_z(dz).wait_send()
+
+
+def kernel_body(hidden, keep_order, keep_count, positions, w_query, w_keyval, cache):
+    scaled, wrapped = rope_table(HD)
+    sign = jnp.asarray([-1.0] * (HD // 2) + [1.0] * (HD // 2), jnp.float32)
+    table = jnp.stack(
+        [jnp.concatenate([scaled, scaled]), jnp.concatenate([wrapped, wrapped]), sign]
+        + [jnp.zeros((HD,), jnp.float32)] * 5
+    )
+    smem = pl.BlockSpec(memory_space=pltpu.SMEM)
+    vmem = pl.BlockSpec(memory_space=pltpu.VMEM)
+    anywhere = pl.BlockSpec(memory_space=pl.ANY)
+    tokens = cache.shape[0]
+    bf16 = jnp.bfloat16
+    dma = pltpu.SemaphoreType.DMA
+    return pl.pallas_call(
+        kernel,
+        out_shape=jax.ShapeDtypeStruct((KEEP, 4 * HD), bf16),
+        in_specs=[smem, smem, smem, vmem, anywhere, anywhere, anywhere, anywhere],
+        out_specs=vmem,
+        scratch_shapes=[
+            pltpu.VMEM(hidden.shape, bf16),
+            pltpu.VMEM(w_query.shape, bf16),
+            pltpu.VMEM(w_keyval.shape, bf16),
+            pltpu.VMEM(cache.shape, bf16),
+            pltpu.VMEM((SHARDS, 16, WIDE), bf16),
+            pltpu.VMEM((SHARDS, QROWS + KEEP, HD), bf16),
+            pltpu.VMEM((KVH, HD, tokens), bf16),
+            pltpu.VMEM((KVH, HD, QROWS), jnp.float32),
+            pltpu.VMEM((KVH, 8, QROWS), jnp.float32),
+            pltpu.VMEM((KVH, MSG, QROWS), bf16),
+            pltpu.VMEM((KVH, MSG, QROWS), bf16),
+            pltpu.VMEM((ZS, MSG, QROWS), bf16),
+            pltpu.VMEM((ZS, MSG, QROWS), bf16),
+            pltpu.VMEM((ZS, MSG, QROWS), bf16),
+            pltpu.VMEM((ZS, MSG, QROWS), bf16),
+            dma((4,)),
+            dma((15,)),
+            dma((16,)),
+            dma((15,)),
+            dma((16,)),
+            dma((8,)),
+            dma((8,)),
+            dma((4,)),
+            dma((4,)),
+            dma((4,)),
+            dma((4,)),
+        ],
+        compiler_params=pltpu.CompilerParams(
+            collective_id=0, has_side_effects=True, vmem_limit_bytes=44 * 1024 * 1024
+        ),
+        cost_estimate=pl.CostEstimate(
+            flops=1_500_000_000, bytes_accessed=15_000_000, transcendentals=2_100_000
+        ),
+    )(keep_order, keep_count, positions, table, hidden, w_query, w_keyval, cache)
+
+
 def solution(mesh):
+    use = kernel_body if mesh.shape["ctx"] == 16 else body
     return jax.shard_map(
-        body,
+        use,
         mesh=mesh,
         in_specs=(
             P(("req", "ctx"), None),

time: 214 us -> 56.5 us (0.26)
  blocking collectives: 112 us -> 0 us
  Pallas kernels: 0 us -> 48.1 us
  waiting for transfers between devices: 35 us -> 0 us
  matrix products: 18.6 us -> 0 us
  between operations: 14.5 us -> 0.02 us
  other arithmetic: 11.1 us -> 0 us
  local copies, waits for them, and re-layouts: 18.3 us -> 8.06 us
  starting transfers between devices: 3.71 us -> 0 us
    unnamed x1 -> x0, blocking collectives: 57.9 us -> none
    pallas_call x0 -> x1, Pallas kernels: none -> 48.1 us  [kernel_body(): pl.pallas_call(kernel, out_shape=jax.ShapeDtypeStruct((KEEP, 4 * HD), bf1...]
    all_gather x1 -> x0, waiting for transfers between devices: 35 us -> none  [body(): rows_all = lax.all_gather(slot_rows, 'ctx', axis=0, tiled=True)]
    pmax x1 -> x0, blocking collectives: 30.4 us -> none  [body(): best = lax.pmax(top.astype(jnp.bfloat16), 'ctx').astype(top.dtype)]
    all_gather x1 -> x0, blocking collectives: 23.4 us -> none  [body(): queries = lax.all_gather(query, 'ctx', axis=1, tiled=True)]
    dot_general x18 -> x0, matrix products: 18.6 us -> none  [the longest x8 6.03 us: body(): jnp.einsum('qhd,kd->qhk', q_group, k_group, preferred_element_type=jnp.fl...]
    reduce_sum x10 -> x0, other arithmetic: 6.44 us -> none  [the longest x8 6.26 us: body(): total_list.append(jnp.sum(weights, axis=2))]
    gather x4 -> x0, local copies, waits for them, and re-layouts: 6.08 us -> none  [the longest x1 2.27 us: body(): slot_rows = hidden[order_here]]
  transfers between devices with their start and end apart: 3 -> 0, of which waited for: 1 -> 0; matrix products, arithmetic and copies ran while one was open for 3% -> 0% of each run, Pallas kernels for 0% -> 0%
where the time goes in v1:
time: 56.5 us; the launch traced here: 56.2 us
  Pallas kernels  48.1 us (85%)
  local copies, waits for them, and re-layouts  8.06 us (14%)
    pallas_call x1, Pallas kernels, kernel_body(): pl.pallas_call(kernel, out_shape=jax.ShapeDtypeStruct((KEEP, 4 * HD), bf1...  48.1 us
    unnamed x15, local copies, waits for them, and re-layouts  8.06 us

profile of v1, /device:TPU:0, one launch (start us, length us, event | category | flops | bytes accessed | tf_op | source)
XLA Modules:
  0.0 56.2 jit_solution(3699677379333995384)
XLA Ops:
  0.0 0.0 copy-start
  0.0 2.2 %copy-done = bf16[1024,2048]{1,0:T(8,128)(2,1)S(1)} copy-done((bf16[1024,2048]{1,0:T(8,128)(2,1)S(1)}, bf16[1024,2048]{1,0:T(8,128)(2,1)}, u32[]{:S(2)}) %copy-start) | copy-done | bytes 4194328
  2.2 0.0 copy-start.1
  2.2 1.6 %copy-done.1 = bf16[8192,128]{1,0:T(8,128)(2,1)S(1)} copy-done((bf16[8192,128]{1,0:T(8,128)(2,1)S(1)}, bf16[8192,128]{1,0:T(8,128)(2,1)}, u32[]{:S(2)}) %copy-start.1) | copy-done | bytes 2097176
  3.8 0.0 copy-start.2
  3.8 0.9 %copy-done.2 = bf16[16,8192]{1,0:T(8,128)(2,1)S(1)} copy-done((bf16[16,8192]{1,0:T(8,128)(2,1)S(1)}, bf16[16,8192]{1,0:T(8,128)(2,1)}, u32[]{:S(2)}) %copy-start.2) | copy-done | bytes 262168
  4.7 0.0 copy-start.3
  4.7 0.7 %copy-done.3 = s32[16,16]{1,0:T(8,128)S(1)} copy-done((s32[16,16]{1,0:T(8,128)S(1)}, s32[16,16]{1,0:T(8,128)}, u32[]{:S(2)}) %copy-start.3) | copy-done | bytes 1048
  5.4 0.0 copy-start.4
  5.4 0.7 %copy-done.4 = f32[8,128]{1,0:T(8,128)S(1)} copy-done((f32[8,128]{1,0:T(8,128)S(1)}, f32[8,128]{1,0:T(8,128)}, u32[]{:S(2)}) %copy-start.4) | copy-done | bytes 4120
  6.1 0.0 copy-start.5
  6.1 0.7 %copy-done.5 = s32[256]{0:T(256)S(1)} copy-done((s32[256]{0:T(256)S(1)}, s32[256]{0:T(256)}, u32[]{:S(2)}) %copy-start.5) | copy-done | bytes 1048
  6.8 0.0 copy-start.6
  6.8 0.7 %copy-done.6 = s32[16]{0:T(128)S(1)} copy-done((s32[16]{0:T(128)S(1)}, s32[16]{0:T(128)}, u32[]{:S(2)}) %copy-start.6) | copy-done | bytes 88
  7.5 48.1 %shard_map.100 = bf16[32,512]{1,0:T(8,128)(2,1)S(1)} custom-call(s32[16,16]{1,0:T(8,128)S(1)} %copy-done.3, s32[16]{0:T(128)S(1)} %copy-done.6, s32[256]{0:T(256)S(1)} %copy-done.5, f32[8,128]{1,0:T(8,128)S(1)} %copy-done.4, bf16[16,8192]{1,0:T(8,128)(2,1)S(1)} %copy-done.2, bf16[8192,512]{1,0:T(8,128)(2,1)} %w_query.1, bf16[8192,128]{1,0:T(8,128)(2,1)S(1)} %copy-done.1, ...), custom_call_target="tpu_custom_call" | custom-call | flops 1500000000 | bytes 15000000 | tf_op jit(solution)/shard_map/pallas_call | solution.py:448
  55.5 0.6 %copy.12 = bf16[32,512]{1,0:T(8,128)(2,1)} copy(bf16[32,512]{1,0:T(8,128)(2,1)S(1)} %shard_map.100) | data formatting | bytes 65536
Async XLA Ops:
  0.0 2.2 %copy-start = (bf16[1024,2048]{1,0:T(8,128)(2,1)S(1)}, bf16[1024,2048]{1,0:T(8,128)(2,1)}, u32[]{:S(2)}) copy-start(bf16[1024,2048]{1,0:T(8,128)(2,1)} %cache.1) | copy-start | bytes 12582916
  2.2 1.6 %copy-start.1 = (bf16[8192,128]{1,0:T(8,128)(2,1)S(1)}, bf16[8192,128]{1,0:T(8,128)(2,1)}, u32[]{:S(2)}) copy-start(bf16[8192,128]{1,0:T(8,128)(2,1)} %w_keyval.1) | copy-start | bytes 6291460
  3.8 0.9 %copy-start.2 = (bf16[16,8192]{1,0:T(8,128)(2,1)S(1)}, bf16[16,8192]{1,0:T(8,128)(2,1)}, u32[]{:S(2)}) copy-start(bf16[16,8192]{1,0:T(8,128)(2,1)} %hidden.1) | copy-start | bytes 786436
  4.7 0.7 %copy-start.3 = (s32[16,16]{1,0:T(8,128)S(1)}, s32[16,16]{1,0:T(8,128)}, u32[]{:S(2)}) copy-start(s32[16,16]{1,0:T(8,128)} %order.1) | copy-start | bytes 3076
  5.4 0.7 %copy-start.4 = (f32[8,128]{1,0:T(8,128)S(1)}, f32[8,128]{1,0:T(8,128)}, u32[]{:S(2)}) copy-start(f32[8,128]{1,0:T(8,128)} %constant.18.table) | copy-start | bytes 12292
  6.1 0.7 %copy-start.5 = (s32[256]{0:T(256)S(1)}, s32[256]{0:T(256)}, u32[]{:S(2)}) copy-start(s32[256]{0:T(256)} %pos.1) | copy-start | bytes 3076
  6.8 0.7 %copy-start.6 = (s32[16]{0:T(128)S(1)}, s32[16]{0:T(128)}, u32[]{:S(2)}) copy-start(s32[16]{0:T(128)} %count.1) | copy-start | bytes 196

commit v2 on v1

--- a/solution.py
+++ b/solution.py
@@ -171,8 +171,8 @@
 
 
 def kernel(
-    order, count, pos, table, hidden, w_query, w_keyval, cache, out,
-    hidden_v, query_v, keyval_v, cache_v, slots, qbuf, values_t,
+    order_h, count_h, pos_h, table_h, hidden, w_query, w_keyval, cache, out,
+    order, count, pos, table, hidden_v, query_v, keyval_v, cache_v, slots, qbuf, values_t,
     own, own_lse, send_s, recv_s, send_y, recv_y, send_z, recv_z,
     load_sem, row_send, row_recv, q_send, q_recv,
     s_send, s_recv, y_send, y_recv, z_send, z_recv,
@@ -200,15 +200,20 @@
         pltpu.make_async_copy(w_query, query_v, load_sem.at[1]),
         pltpu.make_async_copy(w_keyval, keyval_v, load_sem.at[2]),
         pltpu.make_async_copy(cache, cache_v, load_sem.at[3]),
+        pltpu.make_async_copy(order_h, order, load_sem.at[4]),
+        pltpu.make_async_copy(count_h, count, load_sem.at[5]),
+        pltpu.make_async_copy(pos_h, pos, load_sem.at[6]),
+        pltpu.make_async_copy(table_h, table, load_sem.at[7]),
     ]
-    for load in loads:
-        load.start()
+    for at in (4, 0, 5, 6, 7, 3, 1, 2):
+        loads[at].start()
 
     barrier = pltpu.get_barrier_semaphore()
     peers = [sibling, y_peer] + [z_peer(dz) for dz in (1, 2, 3)]
     for peer in peers:
         pl.semaphore_signal(barrier, inc=1, device_id={"ctx": peer}, device_id_type=MESH)
 
+    loads[4].wait()
     row = lax.broadcasted_iota(jnp.int32, (16, 16), 0)
     column = lax.broadcasted_iota(jnp.int32, (16, 16), 1)
     chosen = jnp.zeros((16, 16), jnp.int32)
@@ -222,7 +227,7 @@
     slots[me] = picked.astype(jnp.bfloat16)
     pl.semaphore_wait(barrier, len(peers))
 
-    def relay(buf, send_sem, recv_sem, between):
+    def relay(buf, send_sem, recv_sem):
         sent = []
 
         def send(at, receiver_at, peer):
@@ -247,22 +252,17 @@
                 device_id_type=MESH,
             ).wait_recv()
 
+        def pass_on(dz, dy):
+            arrived(dz, dy, 0)
+            if dy == 0:
+                send((dz, 0, 0), dz * 4 + 2, y_peer)
+            send((dz, dy, 0), dz * 4 + dy * 2 + 1, sibling)
+
         for dz in (2, 1, 3):
             send((0, 0, 0), (ZS - dz) * 4, z_peer(dz))
         send((0, 0, 0), 2, y_peer)
         send((0, 0, 0), 1, sibling)
-        result = between()
-        for dz in (1, 3, 2):
-            arrived(dz, 0, 0)
-            send((dz, 0, 0), dz * 4 + 2, y_peer)
-            send((dz, 0, 0), dz * 4 + 1, sibling)
-        for dz in (0, 1, 3, 2):
-            arrived(dz, 1, 0)
-            send((dz, 1, 0), dz * 4 + 3, sibling)
-        for dy in (0, 1):
-            for dz in (0, 1, 3, 2):
-                arrived(dz, dy, 1)
-        return sent, result
+        return sent, arrived, pass_on
 
     def tables():
         lane = lax.broadcasted_iota(jnp.int32, (1, 256), 1)
@@ -292,12 +292,24 @@
         angle = lower * table[0:1, :] + upper * table[1:2, :]
         return picks, upper * 1024.0 + lower, jnp.cos(angle), jnp.sin(angle) * table[2:3, :]
 
-    def before_rows():
-        result = tables()
-        loads[3].wait()
-        return result
-
-    row_sent, (picks, places, cosine, sine) = relay(slots, row_send, row_recv, before_rows)
+    def transpose(g):
+        at = (KVH + g) * HD
+        values_t[g] = cache_v[:, at : at + HD].T
+
+    row_sent, row_arrived, row_pass = relay(slots, row_send, row_recv)
+    for at in (5, 6, 7):
+        loads[at].wait()
+    picks, places, cosine, sine = tables()
+    loads[3].wait()
+    filler = 0
+    for dz, dy in ((0, 1), (1, 0), (3, 0), (2, 0), (1, 1), (3, 1), (2, 1)):
+        row_pass(dz, dy)
+        transpose(filler)
+        filler += 1
+    transpose(filler)
+    for dy in (0, 1):
+        for dz in (0, 1, 3, 2):
+            row_arrived(dz, dy, 1)
     loads[1].wait()
     loads[2].wait()
     query = jnp.zeros((KEEP, 4 * HD), jnp.float32)
@@ -317,12 +329,7 @@
     plain = keyval.astype(jnp.bfloat16).astype(jnp.float32)
     qbuf[me, QROWS:, :] = jnp.where(me < KVH, turn(plain), plain).astype(jnp.bfloat16)
 
-    def before_queries():
-        for g in range(KVH):
-            at = (KVH + g) * HD
-            values_t[g] = cache_v[:, at : at + HD].T
-
-    q_sent, _ = relay(qbuf, q_send, q_recv, before_queries)
+    q_sent, q_arrived, q_pass = relay(qbuf, q_send, q_recv)
 
     def attend(g):
         keys = cache_v[:, pl.ds(pl.multiple_of(g * HD, HD), HD)]
@@ -366,7 +373,8 @@
         to_sibling(dz, dy).wait_recv()
         return [(own[g], own_lse[g, 0:1, :]), unpack(recv_s, g)]
 
-    turns = [(dz, dy) for dz in (2, 1, 3, 0) for dy in (1, 0)]
+    turns = [(0, 1), (1, 1), (1, 0), (3, 1), (3, 0), (2, 1), (2, 0), (0, 0)]
+    passes = {0: ((0, 1), (1, 0), (3, 0)), 1: ((2, 0), (1, 1), (3, 1)), 2: ((2, 1),)}
 
     def follow(dz, dy):
         if dy == 1:
@@ -387,6 +395,9 @@
     for step in range(len(turns) + lag):
         if step < len(turns):
             dz, dy = turns[step]
+            for link in passes.get(step, ()):
+                q_pass(*link)
+            q_arrived(dz, dy, 1)
             attend(z_at(dz) * 2 + (y if dy == 0 else 1 - y))
             to_sibling(dz, dy).start()
         if step == len(turns) - 1:
@@ -439,18 +450,21 @@
         [jnp.concatenate([scaled, scaled]), jnp.concatenate([wrapped, wrapped]), sign]
         + [jnp.zeros((HD,), jnp.float32)] * 5
     )
-    smem = pl.BlockSpec(memory_space=pltpu.SMEM)
     vmem = pl.BlockSpec(memory_space=pltpu.VMEM)
-    anywhere = pl.BlockSpec(memory_space=pl.ANY)
+    hbm = pl.BlockSpec(memory_space=pltpu.HBM)
     tokens = cache.shape[0]
     bf16 = jnp.bfloat16
     dma = pltpu.SemaphoreType.DMA
     return pl.pallas_call(
         kernel,
         out_shape=jax.ShapeDtypeStruct((KEEP, 4 * HD), bf16),
-        in_specs=[smem, smem, smem, vmem, anywhere, anywhere, anywhere, anywhere],
+        in_specs=[hbm] * 8,
         out_specs=vmem,
         scratch_shapes=[
+            pltpu.SMEM(keep_order.shape, jnp.int32),
+            pltpu.SMEM(keep_count.shape, jnp.int32),
+            pltpu.SMEM(positions.shape, jnp.int32),
+            pltpu.VMEM(table.shape, jnp.float32),
             pltpu.VMEM(hidden.shape, bf16),
             pltpu.VMEM(w_query.shape, bf16),
             pltpu.VMEM(w_keyval.shape, bf16),
@@ -466,7 +480,7 @@
             pltpu.VMEM((ZS, MSG, QROWS), bf16),
             pltpu.VMEM((ZS, MSG, QROWS), bf16),
             pltpu.VMEM((ZS, MSG, QROWS), bf16),
-            dma((4,)),
+            dma((8,)),
             dma((15,)),
             dma((16,)),
             dma((15,)),
@@ -479,7 +493,7 @@
             dma((4,)),
         ],
         compiler_params=pltpu.CompilerParams(
-            collective_id=0, has_side_effects=True, vmem_limit_bytes=44 * 1024 * 1024
+            collective_id=0, has_side_effects=True, vmem_limit_bytes=64 * 1024 * 1024 - 64 * 1024
         ),
         cost_estimate=pl.CostEstimate(
             flops=1_500_000_000, bytes_accessed=15_000_000, transcendentals=2_100_000

time: 56.5 us -> 48.3 us (0.85)
  local copies, waits for them, and re-layouts: 8.06 us -> 1.38 us
  Pallas kernels: 48.1 us -> 46.7 us
    unnamed x15 -> x1, local copies, waits for them, and re-layouts: 8.06 us -> 1.38 us
    pallas_call x1, Pallas kernels: 48.1 us -> 46.7 us  [kernel_body(): pl.pallas_call(kernel, out_shape=jax.ShapeDtypeStruct((KEEP, 4 * HD), bf1...]
where the time goes in v2:
time: 48.3 us; the launch traced here: 48.1 us
  Pallas kernels  46.7 us (97%)
  local copies, waits for them, and re-layouts  1.38 us (3%)
    pallas_call x1, Pallas kernels, kernel_body(): pl.pallas_call(kernel, out_shape=jax.ShapeDtypeStruct((KEEP, 4 * HD), bf1...  46.7 us
    unnamed x1, local copies, waits for them, and re-layouts  1.38 us

profile of v2, /device:TPU:0, one launch (start us, length us, event | category | flops | bytes accessed | tf_op | source)
XLA Modules:
  0.0 48.1 jit_solution(17341815470485619340)
XLA Ops:
  0.0 46.7 %shard_map.100 = bf16[32,512]{1,0:T(8,128)(2,1)} custom-call(s32[16,16]{1,0:T(8,128)} %order_h.1, s32[16]{0:T(128)} %count_h.1, s32[256]{0:T(256)} %pos_h.1, f32[8,128]{1,0:T(8,128)} %constant.18.table_h, bf16[16,8192]{1,0:T(8,128)(2,1)} %hidden.1, bf16[8192,512]{1,0:T(8,128)(2,1)} %w_query.1, bf16[8192,128]{1,0:T(8,128)(2,1)} %w_keyval.1, ...), custom_call_target="tpu_custom_call" | custom-call | flops 1500000000 | bytes 15000000 | tf_op jit(solution)/shard_map/pallas_call | solution.py:458
  46.7 1.4 %copy.12 = bf16[32,512]{1,0:T(8,128)(2,1)} copy(bf16[32,512]{1,0:T(8,128)(2,1)} %shard_map.100) | data formatting | bytes 65536

commit v3 on v2

--- a/solution.py
+++ b/solution.py
@@ -138,6 +138,24 @@
 GROUPS = 4
 WIDE = 2048
 QROWS = 128
+SCHEDULE = (
+    (0, 1, 0),
+    (1, 0, 0),
+    (3, 0, 0),
+    (1, 1, 0),
+    (3, 1, 0),
+    (0, 1, 1),
+    (2, 1, 0),
+    (1, 1, 1),
+    (2, 0, 0),
+    (3, 1, 1),
+    (0, 0, 0),
+    (2, 1, 1),
+    (1, 0, 1),
+    (3, 0, 1),
+    (2, 0, 1),
+    (0, 0, 1),
+)
 EXP2_SCALE = math.log2(math.e) / math.sqrt(HD)
 MSG = QROWS + 16
 
@@ -373,8 +391,8 @@
         to_sibling(dz, dy).wait_recv()
         return [(own[g], own_lse[g, 0:1, :]), unpack(recv_s, g)]
 
-    turns = [(0, 1), (1, 1), (1, 0), (3, 1), (3, 0), (2, 1), (2, 0), (0, 0)]
-    passes = {0: ((0, 1), (1, 0), (3, 0)), 1: ((2, 0), (1, 1), (3, 1)), 2: ((2, 1),)}
+    turns = [(dz, dy) for dz in range(ZS) for dy in (0, 1)]
+    passes = {0: ((0, 1), (1, 0), (3, 0)), 1: ((2, 0),), 3: ((1, 1), (3, 1), (2, 1))}
 
     def follow(dz, dy):
         if dy == 1:
@@ -390,32 +408,37 @@
         to_z(dz).start()
         return None
 
-    lag = 1
+    def fresh_keys():
+        new_keys = qbuf[me // 2, QROWS:, :]
+        new_values = qbuf[KVH + me // 2, QROWS:, :]
+        spot = lax.broadcasted_iota(jnp.int32, (KEEP, QROWS), 0)
+        lane = lax.broadcasted_iota(jnp.int32, (KEEP, QROWS), 1)
+        asker = jnp.sum(jnp.where(lane % KEEP == spot, places, 0.0), axis=0, keepdims=True)
+        scores = contract(new_keys, qbuf[me, :QROWS, :], (1, 1))
+        seen = places <= asker
+        scores = jnp.where(seen, scores, -1e30)
+        top = jnp.max(scores, axis=0, keepdims=True)
+        weights = jnp.where(seen, jnp.exp2((scores - top) * EXP2_SCALE), 0.0)
+        total = jnp.sum(weights, axis=0, keepdims=True)
+        numer = contract(new_values, weights.astype(jnp.bfloat16), (0, 0))
+        fresh = (numer * (1.0 / total), top * EXP2_SCALE + jnp.log2(total))
+        return fresh
+
     local = None
-    for step in range(len(turns) + lag):
-        if step < len(turns):
-            dz, dy = turns[step]
-            for link in passes.get(step, ()):
-                q_pass(*link)
-            q_arrived(dz, dy, 1)
-            attend(z_at(dz) * 2 + (y if dy == 0 else 1 - y))
-            to_sibling(dz, dy).start()
-        if step == len(turns) - 1:
-            new_keys = qbuf[me // 2, QROWS:, :]
-            new_values = qbuf[KVH + me // 2, QROWS:, :]
-            spot = lax.broadcasted_iota(jnp.int32, (KEEP, QROWS), 0)
-            lane = lax.broadcasted_iota(jnp.int32, (KEEP, QROWS), 1)
-            asker = jnp.sum(jnp.where(lane % KEEP == spot, places, 0.0), axis=0, keepdims=True)
-            scores = contract(new_keys, qbuf[me, :QROWS, :], (1, 1))
-            seen = places <= asker
-            scores = jnp.where(seen, scores, -1e30)
-            top = jnp.max(scores, axis=0, keepdims=True)
-            weights = jnp.where(seen, jnp.exp2((scores - top) * EXP2_SCALE), 0.0)
-            total = jnp.sum(weights, axis=0, keepdims=True)
-            numer = contract(new_values, weights.astype(jnp.bfloat16), (0, 0))
-            fresh = (numer * (1.0 / total), top * EXP2_SCALE + jnp.log2(total))
-        if step >= lag:
-            local = follow(*turns[step - lag])
+    fresh = None
+    attended = 0
+    for dz, dy, done in SCHEDULE:
+        if done:
+            local = follow(dz, dy)
+            continue
+        for link in passes.get(attended, ()):
+            q_pass(*link)
+        q_arrived(dz, dy, 1)
+        attend(z_at(dz) * 2 + (y if dy == 0 else 1 - y))
+        to_sibling(dz, dy).start()
+        attended += 1
+        if attended == KVH:
+            fresh = fresh_keys()
 
     pieces = [local, fresh]
     for dz in (1, 3, 2):

time: 48.3 us -> 43.7 us (0.905)
  Pallas kernels: 46.7 us -> 42.1 us
    pallas_call x1, Pallas kernels: 46.7 us -> 42.1 us  [kernel_body(): pl.pallas_call(kernel, out_shape=jax.ShapeDtypeStruct((KEEP, 4 * HD), bf1...]
where the time goes in v3:
time: 43.7 us; the launch traced here: 43.5 us
  Pallas kernels  42.1 us (96%)
  local copies, waits for them, and re-layouts  1.38 us (3%)
    pallas_call x1, Pallas kernels, kernel_body(): pl.pallas_call(kernel, out_shape=jax.ShapeDtypeStruct((KEEP, 4 * HD), bf1...  42.1 us
    unnamed x1, local copies, waits for them, and re-layouts  1.38 us

profile of v3, /device:TPU:0, one launch (start us, length us, event | category | flops | bytes accessed | tf_op | source)
XLA Modules:
  0.0 43.5 jit_solution(7183118028092161326)
XLA Ops:
  0.0 42.1 %shard_map.100 = bf16[32,512]{1,0:T(8,128)(2,1)} custom-call(s32[16,16]{1,0:T(8,128)} %order_h.1, s32[16]{0:T(128)} %count_h.1, s32[256]{0:T(256)} %pos_h.1, f32[8,128]{1,0:T(8,128)} %constant.18.table_h, bf16[16,8192]{1,0:T(8,128)(2,1)} %hidden.1, bf16[8192,512]{1,0:T(8,128)(2,1)} %w_query.1, bf16[8192,128]{1,0:T(8,128)(2,1)} %w_keyval.1, ...), custom_call_target="tpu_custom_call" | custom-call | flops 1500000000 | bytes 15000000 | tf_op jit(solution)/shard_map/pallas_call | solution.py:481
  42.1 1.4 %copy.12 = bf16[32,512]{1,0:T(8,128)(2,1)} copy(bf16[32,512]{1,0:T(8,128)(2,1)} %shard_map.100) | data formatting | bytes 65536

commit v4 on v3

--- a/solution.py
+++ b/solution.py
@@ -276,10 +276,10 @@
                 send((dz, 0, 0), dz * 4 + 2, y_peer)
             send((dz, dy, 0), dz * 4 + dy * 2 + 1, sibling)
 
-        for dz in (2, 1, 3):
-            send((0, 0, 0), (ZS - dz) * 4, z_peer(dz))
         send((0, 0, 0), 2, y_peer)
         send((0, 0, 0), 1, sibling)
+        for dz in (1, 3, 2):
+            send((0, 0, 0), (ZS - dz) * 4, z_peer(dz))
         return sent, arrived, pass_on
 
     def tables():

time: 43.7 us -> 42.6 us (0.975)
  Pallas kernels: 42.1 us -> 41 us
    pallas_call x1, Pallas kernels: 42.1 us -> 41 us  [kernel_body(): pl.pallas_call(kernel, out_shape=jax.ShapeDtypeStruct((KEEP, 4 * HD), bf1...]
where the time goes in v4:
time: 42.6 us; the launch traced here: 42.4 us
  Pallas kernels  41 us (96%)
  local copies, waits for them, and re-layouts  1.38 us (3%)
    pallas_call x1, Pallas kernels, kernel_body(): pl.pallas_call(kernel, out_shape=jax.ShapeDtypeStruct((KEEP, 4 * HD), bf1...  41 us
    unnamed x1, local copies, waits for them, and re-layouts  1.38 us

profile of v4, /device:TPU:0, one launch (start us, length us, event | category | flops | bytes accessed | tf_op | source)
XLA Modules:
  0.0 42.4 jit_solution(17540234203510617836)
XLA Ops:
  0.0 41.0 %shard_map.100 = bf16[32,512]{1,0:T(8,128)(2,1)} custom-call(s32[16,16]{1,0:T(8,128)} %order_h.1, s32[16]{0:T(128)} %count_h.1, s32[256]{0:T(256)} %pos_h.1, f32[8,128]{1,0:T(8,128)} %constant.18.table_h, bf16[16,8192]{1,0:T(8,128)(2,1)} %hidden.1, bf16[8192,512]{1,0:T(8,128)(2,1)} %w_query.1, bf16[8192,128]{1,0:T(8,128)(2,1)} %w_keyval.1, ...), custom_call_target="tpu_custom_call" | custom-call | flops 1500000000 | bytes 15000000 | tf_op jit(solution)/shard_map/pallas_call | solution.py:481
  41.0 1.4 %copy.12 = bf16[32,512]{1,0:T(8,128)(2,1)} copy(bf16[32,512]{1,0:T(8,128)(2,1)} %shard_map.100) | data formatting | bytes 65536

commit v5 on v4

--- a/solution.py
+++ b/solution.py
@@ -392,7 +392,7 @@
         return [(own[g], own_lse[g, 0:1, :]), unpack(recv_s, g)]
 
     turns = [(dz, dy) for dz in range(ZS) for dy in (0, 1)]
-    passes = {0: ((0, 1), (1, 0), (3, 0)), 1: ((2, 0),), 3: ((1, 1), (3, 1), (2, 1))}
+    passes = {0: ((0, 1), (1, 0), (3, 0), (2, 0)), 3: ((1, 1), (3, 1), (2, 1))}
 
     def follow(dz, dy):
         if dy == 1:

time: 42.6 us -> 42.6 us (level)
  no operation moved by 1% of the time
where the time goes in v5:
time: 42.6 us; the launch traced here: 42.4 us
  Pallas kernels  41 us (96%)
  local copies, waits for them, and re-layouts  1.38 us (3%)
    pallas_call x1, Pallas kernels, kernel_body(): pl.pallas_call(kernel, out_shape=jax.ShapeDtypeStruct((KEEP, 4 * HD), bf1...  41 us
    unnamed x1, local copies, waits for them, and re-layouts  1.38 us

profile of v5, /device:TPU:0, one launch (start us, length us, event | category | flops | bytes accessed | tf_op | source)
XLA Modules:
  0.0 42.4 jit_solution(2418256745667580214)
XLA Ops:
  0.0 41.0 %shard_map.100 = bf16[32,512]{1,0:T(8,128)(2,1)} custom-call(s32[16,16]{1,0:T(8,128)} %order_h.1, s32[16]{0:T(128)} %count_h.1, s32[256]{0:T(256)} %pos_h.1, f32[8,128]{1,0:T(8,128)} %constant.18.table_h, bf16[16,8192]{1,0:T(8,128)(2,1)} %hidden.1, bf16[8192,512]{1,0:T(8,128)(2,1)} %w_query.1, bf16[8192,128]{1,0:T(8,128)(2,1)} %w_keyval.1, ...), custom_call_target="tpu_custom_call" | custom-call | flops 1500000000 | bytes 15000000 | tf_op jit(solution)/shard_map/pallas_call | solution.py:481
  41.0 1.4 %copy.12 = bf16[32,512]{1,0:T(8,128)(2,1)} copy(bf16[32,512]{1,0:T(8,128)(2,1)} %shard_map.100) | data formatting | bytes 65536
